TPU v7x, 32 devices: a whole 2x2x4 slice. The times are simulated.
32 devices in a mesh: prow: 4 (over y, x), pcol: 8 (over z, core).
Axes of the slice: x: 2, y: 2, z: 4, core: 2. Of those that a mesh axis runs over, the one named last changes fastest.
Arguments:
- matrix: float32 [2, 14336, 14336], P(None, 'pcol', 'prow'), may hold values from -6 to 6
- panel_lower: float32 [2, 64, 14336], P(None, None, ('prow', 'pcol')), may hold values from -0.75 to 0.75
- pivot_rows: int32 [64], replicated, may hold values from 0 to 14335, as said below
Outputs:
- updated: float32 [2, 14336, 14336], P(None, 'pcol', 'prow')
Inputs may be any that keep to these rules, and one draw needn't show every extreme that they name: pivot_rows[k] lies between k and 14335; some entry equals 14335.
All inputs are finite; a program needn't handle non-finite values.
Results may differ from a plain program's by a relative error of at most 0.0001.
Values sent between devices are 32-bit elements; how exact they have to be, the bound alone decides.
A program may use at most 320 MiB of HBM per device.

v0:
```python
import jax
import jax.numpy as jnp
from jax import lax
from jax.sharding import PartitionSpec as P


def from_root(x, axis, root):
    mine = lax.axis_index(axis) == root
    return lax.psum(jnp.where(mine, x, jnp.zeros_like(x)), axis)


def precise(left, right):
    return jnp.dot(left, right, precision=lax.Precision.HIGHEST, preferred_element_type=jnp.float32)


def complex_product(left, right):
    real_part = precise(left[0], right[0]) - precise(left[1], right[1])
    imag_part = precise(left[0], right[1]) + precise(left[1], right[0])
    return jnp.stack([real_part, imag_part])


def unit_lower_inverse(block):
    width = block.shape[1]
    strict = block * jnp.tril(jnp.ones((width, width), jnp.float32), -1)[None]
    ident = jnp.stack([jnp.eye(width, dtype=jnp.float32), jnp.zeros((width, width), jnp.float32)])
    inverse = ident - strict
    power = strict
    for section in range(1, max(1, (width - 1).bit_length())):
        power = complex_product(power, power)
        inverse = complex_product(inverse, ident + power)
    return inverse


def apply_swaps(pivot_rows, length):

    def one_swap(position, order_map):
        target = pivot_rows[position]
        first = order_map[position]
        second = order_map[target]
        return order_map.at[position].set(second).at[target].set(first)

    return lax.fori_loop(0, pivot_rows.shape[0], one_swap, jnp.arange(length, dtype=jnp.int32))


def on_device(matrix, panel_lower, pivot_rows):
    row_count = matrix.shape[2]
    panel_width = pivot_rows.shape[0]
    row_index = lax.axis_index("prow")
    row_base = row_index * row_count
    on_first = row_index == 0
    order_map = apply_swaps(pivot_rows, row_count * lax.axis_size("prow"))
    touched = jnp.concatenate([jnp.arange(panel_width, dtype=jnp.int32), pivot_rows])
    sources = jnp.take(order_map, touched)
    owned = (sources >= row_base) & (sources < row_base + row_count)
    local_source = jnp.clip(sources - row_base, 0, row_count - 1)
    picked = jnp.where(owned[None, None, :], jnp.take(matrix, local_source, axis=2), 0.0)
    gathered = lax.all_gather(panel_lower, "pcol", axis=2, tiled=True)
    slab = lax.psum(picked, "prow")
    inverse = unit_lower_inverse(jnp.swapaxes(gathered[:, :, :panel_width], 1, 2))
    upper = complex_product(slab[:, :, :panel_width], jnp.swapaxes(inverse, 1, 2))
    upper = from_root(upper, "prow", 0)
    in_mine = (touched >= row_base) & (touched < row_base + row_count)
    target_local = jnp.where(in_mine, touched - row_base, row_count)
    swapped = matrix.at[:, :, target_local].set(slab, mode="drop")
    result = swapped - complex_product(upper, gathered)
    top_piece = jnp.where(on_first, upper, result[:, :, :panel_width])
    return lax.dynamic_update_slice_in_dim(result, top_piece, 0, 2)


def solution(mesh):
    return jax.shard_map(
        on_device,
        mesh=mesh,
        in_specs=(P(None, "pcol", "prow"), P(None, None, ("prow", "pcol")), P()),
        out_specs=P(None, "pcol", "prow"),
        check_vma=False,
    )
```

profile of v0, /device:TPU:0, one launch (start us, length us, event | category | flops | bytes accessed | tf_op | source)
XLA Modules:
  0.0 767.6 jit_solution(1585795750562754207)
XLA Ops:
  8.1 332.4 %while.15 = (s32[]{:T(128)}, s32[14336]{0:T(1024)S(1)}, s32[64]{0:T(128)}, s32[]{:T(128)}, s32[]{:T(128)}, /*index=5*/s32[]{:T(128)}, s32[]{:T(128)}) while((s32[]{:T(128)}, s32[14336]{0:T(1024)S(1)}, s32[64]{0:T(128)}, s32[]{:T(128)}, s32[]{:T(128)}, /*index=5*/s32[]{:T(128)}, s32[]{:T(128)}) %tuple.52), condition=%wide.region_1.2_spmd, body=%wide.region_0.1_spmd.sunk | while | flops 13 | bytes 2255 | solution.py:42
  19.1 1.2 dynamic_slice.23
  24.3 1.2 dynamic_slice.23
  29.5 1.2 dynamic_slice.23
  34.7 1.2 dynamic_slice.23
  39.9 1.2 dynamic_slice.23
  45.1 1.2 dynamic_slice.23
  50.3 1.2 dynamic_slice.23
  55.5 1.2 dynamic_slice.23
  76.3 1.2 dynamic_slice.23
  81.5 1.2 dynamic_slice.23
  86.6 1.2 dynamic_slice.23
  91.8 1.2 dynamic_slice.23
  97.0 1.2 dynamic_slice.23
  102.2 1.2 dynamic_slice.23
  107.4 1.2 dynamic_slice.23
  128.2 1.2 dynamic_slice.23
  133.4 1.2 dynamic_slice.23
  343.2 74.3 %copy.14 = f32[2,1792,3584]{1,0,2:T(2,128)} copy(f32[2,1792,3584]{2,1,0:T(8,128)} %param.9) | data formatting | bytes 102760448 | tf_op args[0]
  417.5 5.2 gather_fusion.1
  422.7 2.6 select_bitcast_fusion
  426.5 69.1 %all-reduce.4.cloned.1.call-done = f32[2,1792,128]{1,0,2:T(2,128)} async-done(((f32[2,1792,128]{1,0,2:T(2,128)}), f32[2,1792,128]{1,0,2:T(2,128)}) %all-reduce.4.cloned.1.call-update) | async-done | bytes 1835024 | tf_op jit(solution)/shard_map/psum | solution.py:58
  495.6 2.2 fusion.37
  508.9 16.6 %scatter_fusion = f32[2,1792,3584]{1,0,2:T(2,128)} fusion(f32[2,1792,3584]{1,0,2:T(2,128)} %copy.14, s32[128]{0:T(128)S(1)} %get-tuple-element.131, f32[128,2,1792]{2,1,0:T(2,128)S(1)} %bitcast.195), kind=kCustom, calls=%fused_computation.2 | custom fusion | bytes 5505536 | tf_op jit(solution)/shard_map/scatter | solution.py:64
  525.5 34.1 %all-reduce.6.cloned.1.call-done = f32[2,1792,64]{1,2,0:T(8,128)} async-done(((f32[2,1792,64]{1,2,0:T(8,128)}), f32[2,1792,64]{1,2,0:T(8,128)}) %all-reduce.6.cloned.1.call-update) | async-done | bytes 917520 | tf_op jit(solution)/shard_map/psum | solution.py:9
  559.6 24.6 %fusion.3 = f32[1792,3584]{0,1:T(8,128)} fusion(f32[2,64,3584]{1,2,0:T(8,128)} %all-gather.2.cloned.1.call-done, f32[2,1792,64]{1,2,0:T(8,128)} %all-reduce.6.cloned.1.call-done), kind=kOutput, calls=%fused_computation.16 | convolution fusion | flops 4932501504 | bytes 27983872 | tf_op jit(solution)/shard_map/dot_general | solution.py:13
  584.2 23.3 %fusion.2 = f32[1792,3584]{0,1:T(8,128)} fusion(f32[2,64,3584]{1,2,0:T(8,128)S(1)} %copy-done, f32[2,1792,64]{1,2,0:T(8,128)S(1)} %copy-done.1), kind=kOutput, calls=%fused_computation.15 | convolution fusion | flops 4932501504 | bytes 27983872 | tf_op jit(solution)/shard_map/dot_general | solution.py:13
  607.5 25.9 %add_bitcast_fusion = f32[1,1792,3584]{1,2,0:T(8,128)} fusion(f32[1792,3584]{0,1:T(8,128)} %fusion.3, f32[2,64,3584]{1,2,0:T(8,128)S(1)} %copy-done, f32[2,1792,64]{1,2,0:T(8,128)S(1)} %copy-done.1), kind=kOutput, calls=%fused_computation.6 | convolution fusion | flops 4938924032 | bytes 53673984 | tf_op jit(solution)/shard_map/dot_general | solution.py:13
  633.4 25.9 %subtract_bitcast_fusion = f32[1,1792,3584]{1,2,0:T(8,128)} fusion(f32[1792,3584]{0,1:T(8,128)} %fusion.2, f32[2,64,3584]{1,2,0:T(8,128)S(1)} %copy-done, f32[2,1792,64]{1,2,0:T(8,128)S(1)} %copy-done.1), kind=kOutput, calls=%fused_computation.7 | convolution fusion | flops 4938924032 | bytes 53673984 | tf_op jit(solution)/shard_map/dot_general | solution.py:13
  659.4 49.4 %maximum_subtract_fusion = f32[2,1792,3584]{1,2,0:T(8,128)} fusion(f32[1,1792,3584]{1,2,0:T(8,128)} %add_bitcast_fusion, f32[1,1792,3584]{1,2,0:T(8,128)} %subtract_bitcast_fusion, f32[2,1792,3584]{1,0,2:T(2,128)} %scatter_fusion), kind=kLoop, calls=%fused_computation.5 | loop fusion | flops 25690112 | bytes 154140672 | tf_op jit(solution)/shard_map/sub | solution.py:65
  708.7 2.2 fusion.8
  711.0 49.2 %copy.21 = f32[2,1792,3584]{2,1,0:T(8,128)} copy(f32[2,1792,3584]{1,2,0:T(8,128)} %fusion.8) | data formatting | bytes 102760448 | tf_op jit(solution)/shard_map/dynamic_update_slice | solution.py:67
  (316 shorter events, 217.8 us)
Async XLA Ops:
  7.4 488.2 %all-reduce.4.cloned.1.call-start = ((), (), s32[]{:S(2)}) async-start(), calls=%async_computation | async-start | bytes 3670016 | tf_op jit(solution)/shard_map/psum | solution.py:58
  422.7 2.7 copy-start.3
  425.3 72.6 %all-gather.2.cloned.1.call-start = ((), (), s32[]{:S(2)}) async-start(), calls=%async_computation.1 | async-start | bytes 4128768 | tf_op jit(solution)/shard_map/all_gather | solution.py:57
  426.3 133.3 %all-reduce.6.cloned.1.call-start = ((), (), s32[]{:S(2)}) async-start(), calls=%async_computation.2 | async-start | bytes 1835008 | tf_op jit(solution)/shard_map/psum | solution.py:9
  505.6 3.3 copy-start.2
  559.6 24.6 %copy-start = (f32[2,64,3584]{1,2,0:T(8,128)S(1)}, f32[2,64,3584]{1,2,0:T(8,128)}, u32[]{:S(2)}) copy-start(f32[2,64,3584]{1,2,0:T(8,128)} %all-gather.2.cloned.1.call-done) | copy-start | bytes 5505028
  559.6 24.6 %copy-start.1 = (f32[2,1792,64]{1,2,0:T(8,128)S(1)}, f32[2,1792,64]{1,2,0:T(8,128)}, u32[]{:S(2)}) copy-start(f32[2,1792,64]{1,2,0:T(8,128)} %all-reduce.6.cloned.1.call-done) | copy-start | bytes 2752516
Sparse Core Ops, SparseCore 0:
  425.4 70.1 all-reduce.3
  509.0 50.6 all-reduce.5
Sparse Core Ops, SparseCore 1:
  427.4 47.3 all-gather.1
where the time goes:
time: 775 us; the launch traced here: 768 us
  local copies, waits for them, and re-layouts  268 us (35%)
  other arithmetic  164 us (21%)
  loops' own time  109 us (14%)
  matrix products  108 us (14%)
  waiting for transfers between devices  103 us (13%)
  between operations  15.3 us (2%)
    another operation x1, loops' own time, apply_swaps(): lax.fori_loop(0, pivot_rows.shape[0], one_swap, jnp.arange(length, dtype=...  109 us
    dot_general x48, matrix products, precise(): jnp.dot(left, right, precision=lax.Precision.HIGHEST, preferred_element_t...  108 us
    scatter x128, other arithmetic, one_swap(): return order_map.at[position].set(second).at[target].set(first)  106 us
    dynamic_slice x64, local copies, waits for them, and re-layouts, one_swap(): target = pivot_rows[position]  79.3 us
    unnamed x10, local copies, waits for them, and re-layouts  75.3 us
    psum x1, waiting for transfers between devices, on_device(): slab = lax.psum(picked, 'prow')  69.1 us
    sub x1, other arithmetic, on_device(): result = swapped - complex_product(upper, gathered)  49.4 us
    dynamic_update_slice x1, local copies, waits for them, and re-layouts, on_device(): return lax.dynamic_update_slice_in_dim(result, top_piece, 0, 2)  49.2 us
  transfers between devices with their start and end apart: 3, of which 2 were waited for; matrix products, arithmetic and copies ran while one was open for 3% of the time, Pallas kernels for 0%

commit v1 on v0

v1 whole, which is shorter than its diff:
```python
import jax
import jax.numpy as jnp
from jax import lax
from jax.experimental import pallas as pl
from jax.experimental.pallas import tpu as pltpu
from jax.sharding import PartitionSpec as P

LANES = 128
MIB = 1 << 20


def largest_divisor(extent, limit, multiple):
    size = multiple
    for candidate in range(multiple, limit + 1, multiple):
        if extent % candidate == 0:
            size = candidate
    return size


def precise(left, right):
    return jnp.dot(left, right, precision=lax.Precision.HIGHEST, preferred_element_type=jnp.float32)


def displaced_rows(pivot_col):
    width = pivot_col.shape[0]
    step = lax.broadcasted_iota(jnp.int32, (width, LANES), 0)
    lane = lax.broadcasted_iota(jnp.int32, (width, LANES), 1)
    earlier = jnp.where((pivot_col == lane) & (step < lane), step, -1)
    latest = jnp.max(earlier, axis=0, keepdims=True)
    latest = jnp.where(latest < 0, lane[:1], latest)
    chain = jnp.broadcast_to(latest, (8, LANES))
    for _ in range(max(1, (width - 1).bit_length())):
        chain = jnp.take_along_axis(chain, chain, axis=1)
    return chain


def wanted_rows(pivot_row, pivot_col):
    width = pivot_col.shape[0]
    step = lax.broadcasted_iota(jnp.int32, (width, LANES), 0)
    lane = lax.broadcasted_iota(jnp.int32, (width, LANES), 1)
    chain = displaced_rows(pivot_col)
    earlier = jnp.where((pivot_col == pivot_row) & (step < lane), step, -1)
    latest = jnp.broadcast_to(jnp.max(earlier, axis=0, keepdims=True), (8, LANES))
    from_chain = jnp.take_along_axis(chain, jnp.maximum(latest, 0), axis=1)
    top = jnp.where(latest < 0, jnp.broadcast_to(pivot_row, (8, LANES)), from_chain)
    lane8 = lax.broadcasted_iota(jnp.int32, (8, LANES), 1)
    return jnp.where(lane8 < width, top, lane8 - width)


def pick_kernel(pivot_row_ref, pivot_col_ref, matrix_ref, picked_ref):
    row_count = matrix_ref.shape[2]
    column_count = matrix_ref.shape[1]
    base = lax.axis_index("prow") * row_count
    local = wanted_rows(pivot_row_ref[...], pivot_col_ref[...]) - base
    owned = (local >= 0) & (local < row_count)
    tile = jnp.where(owned, local // LANES, -1)
    within = jnp.where(owned, local % LANES, 0)
    group = 16
    tile = jnp.concatenate([tile] * (group // 8), axis=0)
    within = jnp.concatenate([within] * (group // 8), axis=0)

    def one_group(g, carry):
        rows = pl.ds(pl.multiple_of(g * group, group), group)
        for part in range(2):
            total = jnp.zeros((group, LANES), jnp.float32)
            for t in range(row_count // LANES):
                block = matrix_ref[part, rows, pl.ds(t * LANES, LANES)]
                total = jnp.where(tile == t, jnp.take_along_axis(block, within, axis=1), total)
            picked_ref[part, rows, :] = total
        return carry

    lax.fori_loop(0, column_count // group, one_group, 0)


def pick(pivot_row, pivot_col, matrix):
    _, columns, rows = matrix.shape
    chunk = largest_divisor(columns, 128, 16)
    return pl.pallas_call(
        pick_kernel,
        out_shape=jax.ShapeDtypeStruct((2, columns, LANES), jnp.float32),
        grid=(columns // chunk,),
        in_specs=[
            pl.BlockSpec(pivot_row.shape, lambda i: (0, 0)),
            pl.BlockSpec(pivot_col.shape, lambda i: (0, 0)),
            pl.BlockSpec((2, chunk, rows), lambda i: (0, i, 0)),
        ],
        out_specs=pl.BlockSpec((2, chunk, LANES), lambda i: (0, i, 0)),
        compiler_params=pltpu.CompilerParams(vmem_limit_bytes=24 * MIB),
        cost_estimate=pl.CostEstimate(flops=columns * rows * 2, bytes_accessed=columns * rows * 8, transcendentals=0),
    )(pivot_row, pivot_col, matrix)


def split(value):
    high = value.astype(jnp.bfloat16)
    return high, (value - high.astype(jnp.float32)).astype(jnp.bfloat16)


def prepare_kernel(pivot_col_ref, slab_ref, corner_ref, panel_ref, left_ref, right_ref, keep_ref):
    width = panel_ref.shape[1]
    row_count = panel_ref.shape[2]
    base = lax.axis_index("prow") * row_count
    up = lax.broadcasted_iota(jnp.int32, (width, width), 0) < lax.broadcasted_iota(jnp.int32, (width, width), 1)
    real = jnp.where(up, corner_ref[0], 0.0)
    imag = jnp.where(up, corner_ref[1], 0.0)
    power = jnp.concatenate(
        [jnp.concatenate([real, imag], axis=1), jnp.concatenate([-imag, real], axis=1)], axis=0
    )
    ident = (
        lax.broadcasted_iota(jnp.int32, power.shape, 0) == lax.broadcasted_iota(jnp.int32, power.shape, 1)
    ).astype(jnp.float32)
    inverse = ident - power
    for _ in range(1, max(1, (width - 1).bit_length())):
        power = precise(power, power)
        inverse = precise(inverse, ident + power)

    chunk = largest_divisor(slab_ref.shape[1], 256, 16)

    def one_chunk(g, carry):
        rows = pl.ds(pl.multiple_of(g * chunk, chunk), chunk)
        parts = [slab_ref[part, rows, :] for part in range(2)]
        top = jnp.concatenate([part[:, :width] for part in parts], axis=1)
        upper_high, upper_low = split(precise(top, inverse))
        left_ref[rows, 0:LANES] = upper_high
        left_ref[rows, LANES : 2 * LANES] = upper_low
        for part in range(2):
            start = (2 + 2 * part) * LANES
            high, low = split(parts[part][:, width:])
            left_ref[rows, start : start + LANES] = upper_high
            left_ref[rows, start + LANES : start + 2 * LANES] = jnp.concatenate([high, low], axis=1)
        return carry

    lax.fori_loop(0, slab_ref.shape[1] // chunk, one_chunk, 0)

    chain = displaced_rows(pivot_col_ref[...])[:1]
    source_is = (
        (lax.broadcasted_iota(jnp.int32, (width, width), 0) == chain[:, :width])
        .astype(jnp.float32)
        .astype(jnp.bfloat16)
    )
    span = largest_divisor(row_count, 512, LANES)

    def one_span(t, carry):
        start = pl.multiple_of(t * span, span)
        lanes = pl.ds(start, span)
        step = lax.broadcasted_iota(jnp.int32, (width, span), 0)
        position = lax.broadcasted_iota(jnp.int32, (width, span), 1) + (start + base)
        latest = jnp.max(jnp.where(pivot_col_ref[...] == position, step, -1), axis=0, keepdims=True)
        at_top = position < width
        moved = (latest == step) & jnp.logical_not(at_top)
        chosen = jnp.dot(
            source_is, moved.astype(jnp.float32).astype(jnp.bfloat16), preferred_element_type=jnp.float32
        ).astype(jnp.bfloat16)
        real = jnp.where(at_top, -(position == step).astype(jnp.float32), panel_ref[0, :, lanes])
        imag = jnp.where(at_top, 0.0, panel_ref[1, :, lanes])
        real_high, real_low = split(real)
        imag_high, imag_low = split(imag)
        for part in range(2):
            if part == 0:
                high = [-real_high, imag_high]
                low = [-real_low, imag_low]
            else:
                high = [-imag_high, -real_high]
                low = [-imag_low, -real_low]
            for index, piece in enumerate(high + high + low + [chosen, chosen]):
                right_ref[part, index * width : (index + 1) * width, lanes] = piece
        keep = (latest < 0) & (position[:1] >= width)
        keep_ref[:, lanes] = jnp.broadcast_to(keep.astype(jnp.float32), (8, span))
        return carry

    lax.fori_loop(0, row_count // span, one_span, 0)


def prepare(pivot_col, slab, corner, panel):
    _, columns, _ = slab.shape
    _, width, rows = panel.shape
    whole = pl.BlockSpec(memory_space=pltpu.VMEM)
    return pl.pallas_call(
        prepare_kernel,
        out_shape=(
            jax.ShapeDtypeStruct((columns, 6 * LANES), jnp.bfloat16),
            jax.ShapeDtypeStruct((2, 8 * width, rows), jnp.bfloat16),
            jax.ShapeDtypeStruct((8, rows), jnp.float32),
        ),
        in_specs=[whole] * 4,
        out_specs=(whole,) * 3,
        compiler_params=pltpu.CompilerParams(vmem_limit_bytes=28 * MIB),
    )(pivot_col, slab, corner, panel)


def update_kernel(left_ref, right_ref, keep_ref, matrix_ref, out_ref):
    columns, rows = matrix_ref.shape[1:]
    half = 2 * LANES
    span = largest_divisor(rows, 256, LANES)
    offset = pl.program_id(1) * rows

    def one_span(t, carry):
        here = pl.ds(pl.multiple_of(t * span, span), span)
        there = pl.ds(pl.multiple_of(offset + t * span, LANES), span)
        keep = keep_ref[:1, there] > 0.5
        for part in range(2):
            product = jnp.dot(
                left_ref[:, 0:half], right_ref[part, 0:half, there], preferred_element_type=jnp.float32
            ) + jnp.dot(
                left_ref[:, (1 + part) * half : (2 + part) * half],
                right_ref[part, half : 2 * half, there],
                preferred_element_type=jnp.float32,
            )
            out_ref[part, :, here] = jnp.where(keep, matrix_ref[part, :, here], 0.0) + product
        return carry

    lax.fori_loop(0, rows // span, one_span, 0)


def update(left, right, keep, matrix):
    _, columns, rows = matrix.shape
    chunk = largest_divisor(columns, 256, 16)
    row_chunk = largest_divisor(rows, 1792, LANES)
    return pl.pallas_call(
        update_kernel,
        out_shape=jax.ShapeDtypeStruct(matrix.shape, jnp.float32),
        grid=(columns // chunk, rows // row_chunk),
        in_specs=[
            pl.BlockSpec((chunk, left.shape[1]), lambda i, j: (i, 0)),
            pl.BlockSpec(right.shape, lambda i, j: (0, 0, 0), pipeline_mode=pl.Buffered(1)),
            pl.BlockSpec(keep.shape, lambda i, j: (0, 0), pipeline_mode=pl.Buffered(1)),
            pl.BlockSpec((2, chunk, row_chunk), lambda i, j: (0, i, j)),
        ],
        out_specs=pl.BlockSpec((2, chunk, row_chunk), lambda i, j: (0, i, j)),
        compiler_params=pltpu.CompilerParams(vmem_limit_bytes=40 * MIB),
    )(left, right, keep, matrix)


def on_device(matrix, panel_lower, pivot_rows):
    width = pivot_rows.shape[0]
    pivot_row = jnp.pad(pivot_rows, (0, LANES - width), constant_values=-1).reshape(1, LANES)
    pivot_col = pivot_rows.reshape(width, 1)
    gathered = lax.all_gather(panel_lower, "pcol", axis=2, tiled=True)
    corner = lax.psum(jnp.where(lax.axis_index("prow") == 0, gathered[:, :, :width], 0.0), "prow")
    picked = pick(pivot_row, pivot_col, matrix)
    slab = lax.psum(picked, "prow")
    left, right, keep = prepare(pivot_col, slab, corner, gathered)
    return update(left, right, keep, matrix)


def solution(mesh):
    return jax.shard_map(
        on_device,
        mesh=mesh,
        in_specs=(P(None, "pcol", "prow"), P(None, None, ("prow", "pcol")), P()),
        out_specs=P(None, "pcol", "prow"),
        check_vma=False,
    )
```

time: 775 us -> 173 us (0.22)
  local copies, waits for them, and re-layouts: 268 us -> 9.22 us
  other arithmetic: 164 us -> 0.02 us
  loops' own time: 109 us -> 0 us
  matrix products: 108 us -> 0 us
  Pallas kernels: 0 us -> 84.1 us
  waiting for transfers between devices: 103 us -> 47 us
  blocking collectives: 0 us -> 16.9 us
    another operation x1 -> x0, loops' own time: 109 us -> none  [apply_swaps(): lax.fori_loop(0, pivot_rows.shape[0], one_swap, jnp.arange(length, dtype=...]
    dot_general x48 -> x0, matrix products: 108 us -> none  [precise(): jnp.dot(left, right, precision=lax.Precision.HIGHEST, preferred_element_t...]
    scatter x128 -> x0, other arithmetic: 106 us -> none  [one_swap(): return order_map.at[position].set(second).at[target].set(first)]
    pallas_call x0 -> x3, Pallas kernels: none -> 84.1 us  [the longest x1 45.2 us: update(): pl.pallas_call(update_kernel, out_shape=jax.ShapeDtypeStruct(matrix.shape...]
    dynamic_slice x64 -> x0, local copies, waits for them, and re-layouts: 79.3 us -> none  [one_swap(): target = pivot_rows[position]]
    unnamed x10 -> x3, local copies, waits for them, and re-layouts: 75.3 us -> 3.45 us
    sub x2 -> x0, other arithmetic: 50.2 us -> none  [the longest x1 49.4 us: on_device(): result = swapped - complex_product(upper, gathered)]
    dynamic_update_slice x1 -> x0, local copies, waits for them, and re-layouts: 49.2 us -> none  [on_device(): return lax.dynamic_update_slice_in_dim(result, top_piece, 0, 2)]
  transfers between devices with their start and end apart: 3 -> 2, of which waited for: 2 -> 2; matrix products, arithmetic and copies ran while one was open for 3% -> 3% of each run, Pallas kernels for 0% -> 19%
where the time goes in v1:
time: 173 us; the launch traced here: 172 us
  Pallas kernels  84.1 us (49%)
  waiting for transfers between devices  47 us (27%)
  blocking collectives  16.9 us (10%)
  between operations  14.9 us (9%)
  local copies, waits for them, and re-layouts  9.22 us (5%)
    pallas_call x1, Pallas kernels, update(): pl.pallas_call(update_kernel, out_shape=jax.ShapeDtypeStruct(matrix.shape...  45.2 us
    psum x1, waiting for transfers between devices, on_device(): slab = lax.psum(picked, 'prow')  34.6 us
    pallas_call x1, Pallas kernels, pick(): pl.pallas_call(pick_kernel, out_shape=jax.ShapeDtypeStruct((2, columns, L...  32.5 us
    psum x1, blocking collectives, on_device(): lax.psum(jnp.where(lax.axis_index('prow') == 0, gathered[:, :, :width], 0...  16.9 us
    all_gather x1, waiting for transfers between devices, on_device(): gathered = lax.all_gather(panel_lower, 'pcol', axis=2, tiled=True)  12.3 us
    pallas_call x1, Pallas kernels, prepare(): pl.pallas_call(prepare_kernel, out_shape=(jax.ShapeDtypeStruct((columns,...  6.35 us
    all_gather x1, local copies, waits for them, and re-layouts, on_device(): gathered = lax.all_gather(panel_lower, 'pcol', axis=2, tiled=True)  4.37 us
  transfers between devices with their start and end apart: 2, of which 2 were waited for; matrix products, arithmetic and copies ran while one was open for 3% of the time, Pallas kernels for 19%

profile of v1, /device:TPU:0, one launch (start us, length us, event | category | flops | bytes accessed | tf_op | source)
XLA Modules:
  0.0 172.2 jit_solution(9206118337150674448)
XLA Ops:
  7.4 0.0 all-gather.2.cloned.1.call-start
  7.4 2.0 %copy.7 = f32[2,64,448]{1,0,2:T(2,128)} copy(f32[2,64,448]{2,1,0:T(8,128)} %param.4) | data formatting | bytes 458752 | tf_op args[1]
  9.3 0.0 all-gather.2.cloned.1.call-update
  9.3 0.0 all-reduce.3.cloned.1.call-start
  9.4 0.7 copy.9.pivot_col_ref
  10.1 0.7 pad_bitcast_fusion.pivot_row_ref
  10.8 32.5 %shard_map.37 = f32[2,1792,128]{2,1,0:T(8,128)} custom-call(s32[1,128]{1,0:T(1,128)S(1)} %pad_bitcast_fusion.pivot_row_ref, s32[64,1]{1,0:T(8,128)S(1)} %copy.9.pivot_col_ref, f32[2,1792,3584]{2,1,0:T(8,128)} %matrix_ref.3), custom_call_target="tpu_custom_call" | custom-call | flops 12845056 | bytes 51380224 | tf_op jit(solution)/shard_map/pallas_call | solution.py:78
  43.3 0.0 all-reduce.3.cloned.1.call-update
  43.4 12.3 %all-gather.2.cloned.1.call-done = f32[2,64,3584]{1,0,2:T(2,128)} async-done(((f32[2,64,448]{1,0,2:T(2,128)}), f32[2,64,3584]{1,0,2:T(2,128)}) %all-gather.2.cloned.1.call-update) | async-done | bytes 1835024 | tf_op jit(solution)/shard_map/all_gather | solution.py:237
  55.7 4.4 %copy.8.panel_ref = f32[2,64,3584]{2,1,0:T(8,128)S(1)} copy(f32[2,64,3584]{1,0,2:T(2,128)} %all-gather.2.cloned.1.call-done) | data formatting | bytes 3670016 | tf_op jit(solution)/shard_map/all_gather | solution.py:237
  60.1 16.9 %psum.15.corner_ref = f32[2,64,64]{2,1,0:T(8,128)S(1)} all-reduce(f32[2,64,64]{2,1,0:T(8,128)S(1)} %slice_select_fusion), channel_id=1, replica_groups=mesh['prow'=4,'pcol'=8] {'prow'}, use_global_device_ids=true, to_apply=%region_1.2 | all-reduce | flops 8192 | bytes 65536 | tf_op jit(solution)/shard_map/psum | solution.py:238
  77.0 34.6 %all-reduce.3.cloned.1.call-done.slab_ref = f32[2,1792,128]{2,1,0:T(8,128)} async-done(((f32[2,1792,128]{2,1,0:T(8,128)}), f32[2,1792,128]{2,1,0:T(8,128)}) %all-reduce.3.cloned.1.call-update) | async-done | bytes 1835024 | tf_op jit(solution)/shard_map/psum | solution.py:240
  111.6 0.0 copy-start
  111.6 1.5 copy-done
  113.1 6.4 %shard_map.38 = (bf16[1792,768]{1,0:T(8,128)(2,1)S(1)}, bf16[2,512,3584]{2,1,0:T(8,128)(2,1)S(1)}, f32[8,3584]{1,0:T(8,128)S(1)}) custom-call(s32[64,1]{1,0:T(8,128)S(1)} %copy.9.pivot_col_ref, f32[2,1792,128]{2,1,0:T(8,128)S(1)} %copy-done, f32[2,64,64]{2,1,0:T(8,128)S(1)} %psum.15.corner_ref, f32[2,64,3584]{2,1,0:T(8,128)S(1)} %copy.8.panel_ref), custom_call_target="tpu_custom_call" | custom-call | tf_op jit(solution)/shard_map/pallas_call | solution.py:177
  119.5 45.2 %shard_map.39 = f32[2,1792,3584]{2,1,0:T(8,128)} custom-call(bf16[1792,768]{1,0:T(8,128)(2,1)S(1)} %get-tuple-element.8.left_ref, bf16[2,512,3584]{2,1,0:T(8,128)(2,1)S(1)} %get-tuple-element.9.right_ref, f32[8,3584]{1,0:T(8,128)S(1)} %get-tuple-element.10.keep_ref, f32[2,1792,3584]{2,1,0:T(8,128)} %matrix_ref.3), custom_call_target="tpu_custom_call" | custom-call | tf_op jit(solution)/shard_map/pallas_call | solution.py:218
  (1 shorter events, 0.0 us)
Async XLA Ops:
  7.4 48.3 %all-gather.2.cloned.1.call-start = ((), (), s32[]{:S(2)}) async-start(), calls=%async_computation.1 | async-start | bytes 4128768 | tf_op jit(solution)/shard_map/all_gather | solution.py:237
  9.3 102.3 %all-reduce.3.cloned.1.call-start = ((), (), s32[]{:S(2)}) async-start(), calls=%async_computation | async-start | bytes 3670016 | tf_op jit(solution)/shard_map/psum | solution.py:240
  111.6 1.5 copy-start
Sparse Core Ops, SparseCore 0:
  9.9 45.6 all-gather.1
Sparse Core Ops, SparseCore 1:
  43.5 68.1 all-reduce.2

commit v2 on v1

--- a/solution.py
+++ b/solution.py
@@ -95,13 +95,13 @@
     return high, (value - high.astype(jnp.float32)).astype(jnp.bfloat16)
 
 
-def prepare_kernel(pivot_col_ref, slab_ref, corner_ref, panel_ref, left_ref, right_ref, keep_ref):
-    width = panel_ref.shape[1]
-    row_count = panel_ref.shape[2]
+def prepare_kernel(pivot_col_ref, top_ref, old_ref, corner_ref, panel_ref, left_ref, right_ref, keep_ref):
+    slots, _, width, share = panel_ref.shape
+    row_count = slots * share
     base = lax.axis_index("prow") * row_count
     up = lax.broadcasted_iota(jnp.int32, (width, width), 0) < lax.broadcasted_iota(jnp.int32, (width, width), 1)
-    real = jnp.where(up, corner_ref[0], 0.0)
-    imag = jnp.where(up, corner_ref[1], 0.0)
+    real = jnp.where(up, corner_ref[:, :width], 0.0)
+    imag = jnp.where(up, corner_ref[:, width:], 0.0)
     power = jnp.concatenate(
         [jnp.concatenate([real, imag], axis=1), jnp.concatenate([-imag, real], axis=1)], axis=0
     )
@@ -113,23 +113,23 @@
         power = precise(power, power)
         inverse = precise(inverse, ident + power)
 
-    chunk = largest_divisor(slab_ref.shape[1], 256, 16)
+    chunk = largest_divisor(top_ref.shape[0], 256, 16)
 
     def one_chunk(g, carry):
         rows = pl.ds(pl.multiple_of(g * chunk, chunk), chunk)
-        parts = [slab_ref[part, rows, :] for part in range(2)]
-        top = jnp.concatenate([part[:, :width] for part in parts], axis=1)
-        upper_high, upper_low = split(precise(top, inverse))
-        left_ref[rows, 0:LANES] = upper_high
-        left_ref[rows, LANES : 2 * LANES] = upper_low
+        upper_high, upper_low = split(precise(top_ref[rows, :], inverse))
+        old_high, old_low = split(old_ref[rows, :])
         for part in range(2):
-            start = (2 + 2 * part) * LANES
-            high, low = split(parts[part][:, width:])
-            left_ref[rows, start : start + LANES] = upper_high
-            left_ref[rows, start + LANES : start + 2 * LANES] = jnp.concatenate([high, low], axis=1)
+            mine = slice(part * width, (part + 1) * width)
+            left_ref[part, rows, 0:LANES] = upper_high
+            left_ref[part, rows, LANES : 2 * LANES] = upper_low
+            left_ref[part, rows, 2 * LANES : 3 * LANES] = upper_high
+            left_ref[part, rows, 3 * LANES : 4 * LANES] = jnp.concatenate(
+                [old_high[:, mine], old_low[:, mine]], axis=1
+            )
         return carry
 
-    lax.fori_loop(0, slab_ref.shape[1] // chunk, one_chunk, 0)
+    lax.fori_loop(0, top_ref.shape[0] // chunk, one_chunk, 0)
 
     chain = displaced_rows(pivot_col_ref[...])[:1]
     source_is = (
@@ -137,21 +137,26 @@
         .astype(jnp.float32)
         .astype(jnp.bfloat16)
     )
-    span = largest_divisor(row_count, 512, LANES)
-
-    def one_span(t, carry):
-        start = pl.multiple_of(t * span, span)
-        lanes = pl.ds(start, span)
+    group = 1
+    while group < slots and (group * share) % LANES:
+        group *= 2
+    span = group * share
+
+    for t in range(slots // group):
+        lanes = slice(t * span, (t + 1) * span)
         step = lax.broadcasted_iota(jnp.int32, (width, span), 0)
-        position = lax.broadcasted_iota(jnp.int32, (width, span), 1) + (start + base)
+        position = lax.broadcasted_iota(jnp.int32, (width, span), 1) + (t * span + base)
         latest = jnp.max(jnp.where(pivot_col_ref[...] == position, step, -1), axis=0, keepdims=True)
         at_top = position < width
         moved = (latest == step) & jnp.logical_not(at_top)
         chosen = jnp.dot(
             source_is, moved.astype(jnp.float32).astype(jnp.bfloat16), preferred_element_type=jnp.float32
         ).astype(jnp.bfloat16)
-        real = jnp.where(at_top, -(position == step).astype(jnp.float32), panel_ref[0, :, lanes])
-        imag = jnp.where(at_top, 0.0, panel_ref[1, :, lanes])
+        pieces = [
+            jnp.concatenate([panel_ref[t * group + g, part] for g in range(group)], axis=1) for part in range(2)
+        ]
+        real = jnp.where(at_top, -(position == step).astype(jnp.float32), pieces[0])
+        imag = jnp.where(at_top, 0.0, pieces[1])
         real_high, real_low = split(real)
         imag_high, imag_low = split(imag)
         for part in range(2):
@@ -165,80 +170,373 @@
                 right_ref[part, index * width : (index + 1) * width, lanes] = piece
         keep = (latest < 0) & (position[:1] >= width)
         keep_ref[:, lanes] = jnp.broadcast_to(keep.astype(jnp.float32), (8, span))
-        return carry
-
-    lax.fori_loop(0, row_count // span, one_span, 0)
-
-
-def prepare(pivot_col, slab, corner, panel):
-    _, columns, _ = slab.shape
-    _, width, rows = panel.shape
+
+
+def prepare(pivot_col, top, old, corner, panel):
+    columns = top.shape[0]
+    slots, _, width, share = panel.shape
+    rows = slots * share
     whole = pl.BlockSpec(memory_space=pltpu.VMEM)
     return pl.pallas_call(
         prepare_kernel,
         out_shape=(
-            jax.ShapeDtypeStruct((columns, 6 * LANES), jnp.bfloat16),
+            jax.ShapeDtypeStruct((2, columns, 4 * LANES), jnp.bfloat16),
             jax.ShapeDtypeStruct((2, 8 * width, rows), jnp.bfloat16),
             jax.ShapeDtypeStruct((8, rows), jnp.float32),
         ),
-        in_specs=[whole] * 4,
+        in_specs=[whole] * 5,
         out_specs=(whole,) * 3,
-        compiler_params=pltpu.CompilerParams(vmem_limit_bytes=28 * MIB),
-    )(pivot_col, slab, corner, panel)
+        compiler_params=pltpu.CompilerParams(vmem_limit_bytes=32 * MIB),
+    )(pivot_col, top, old, corner, panel)
 
 
 def update_kernel(left_ref, right_ref, keep_ref, matrix_ref, out_ref):
-    columns, rows = matrix_ref.shape[1:]
-    half = 2 * LANES
-    span = largest_divisor(rows, 256, LANES)
-    offset = pl.program_id(1) * rows
-
-    def one_span(t, carry):
-        here = pl.ds(pl.multiple_of(t * span, span), span)
-        there = pl.ds(pl.multiple_of(offset + t * span, LANES), span)
-        keep = keep_ref[:1, there] > 0.5
-        for part in range(2):
-            product = jnp.dot(
-                left_ref[:, 0:half], right_ref[part, 0:half, there], preferred_element_type=jnp.float32
-            ) + jnp.dot(
-                left_ref[:, (1 + part) * half : (2 + part) * half],
-                right_ref[part, half : 2 * half, there],
-                preferred_element_type=jnp.float32,
-            )
-            out_ref[part, :, here] = jnp.where(keep, matrix_ref[part, :, here], 0.0) + product
-        return carry
-
-    lax.fori_loop(0, rows // span, one_span, 0)
+    columns = matrix_ref.shape[1]
+    chunk = largest_divisor(columns, 896, 16)
+    keep = keep_ref[:1, :] > 0.5
+    for part in range(2):
+        for start in range(0, columns, chunk):
+            rows = slice(start, start + chunk)
+            product = jnp.dot(left_ref[part, rows, :], right_ref[part], preferred_element_type=jnp.float32)
+            out_ref[part, rows, :] = jnp.where(keep, matrix_ref[part, rows, :], 0.0) + product
 
 
 def update(left, right, keep, matrix):
     _, columns, rows = matrix.shape
-    chunk = largest_divisor(columns, 256, 16)
-    row_chunk = largest_divisor(rows, 1792, LANES)
+    span = largest_divisor(rows, 2 * LANES, LANES)
     return pl.pallas_call(
         update_kernel,
         out_shape=jax.ShapeDtypeStruct(matrix.shape, jnp.float32),
-        grid=(columns // chunk, rows // row_chunk),
+        grid=(rows // span,),
         in_specs=[
-            pl.BlockSpec((chunk, left.shape[1]), lambda i, j: (i, 0)),
-            pl.BlockSpec(right.shape, lambda i, j: (0, 0, 0), pipeline_mode=pl.Buffered(1)),
-            pl.BlockSpec(keep.shape, lambda i, j: (0, 0), pipeline_mode=pl.Buffered(1)),
-            pl.BlockSpec((2, chunk, row_chunk), lambda i, j: (0, i, j)),
+            pl.BlockSpec(left.shape, lambda j: (0, 0, 0), pipeline_mode=pl.Buffered(1)),
+            pl.BlockSpec((2, right.shape[1], span), lambda j: (0, 0, j)),
+            pl.BlockSpec((8, span), lambda j: (0, j)),
+            pl.BlockSpec((2, columns, span), lambda j: (0, 0, j)),
         ],
-        out_specs=pl.BlockSpec((2, chunk, row_chunk), lambda i, j: (0, i, j)),
+        out_specs=pl.BlockSpec((2, columns, span), lambda j: (0, 0, j)),
         compiler_params=pltpu.CompilerParams(vmem_limit_bytes=40 * MIB),
     )(left, right, keep, matrix)
 
 
+def exchange_kernel(
+    peers, ring, pivot_row_ref, pivot_col_ref, corner_ref, panel_ref, matrix_ref,
+    top_ref, old_ref, corner_out_ref, slots_ref,
+    choose, mine, old, inbox, total,
+    rs_send, rs_recv, ag_send, ag_recv, old_send, old_recv, spread_send, spread_recv,
+    panel_send, panel_recv, pass_send, pass_recv, corner_send, corner_recv, local_sem,
+):
+    width = pivot_col_ref.shape[0]
+    _, chunk, row_count = matrix_ref.shape
+    quarter = chunk // peers
+    last = pl.num_programs(0) - 1
+    step = pl.program_id(0)
+    p = lax.axis_index("prow")
+    q = lax.axis_index("pcol")
+    sibling = q + 1 - 2 * lax.rem(q, 2)
+    hops = ring // 2
+
+    def other(d):
+        return lax.rem(p + d, peers)
+
+    def sender(d):
+        return lax.rem(p + peers - d, peers)
+
+    def along(d):
+        return lax.rem(q + 2 * d, ring)
+
+    def behind(d):
+        return lax.rem(q + ring - 2 * d, ring)
+
+    def remote(src, dst, send, recv, row, column):
+        return pltpu.make_async_remote_copy(
+            src_ref=src, dst_ref=dst, send_sem=send, recv_sem=recv,
+            device_id=(row, column), device_id_type=pl.DeviceIdType.MESH,
+        )
+
+    def part_rows(i, owner):
+        return pl.ds(pl.multiple_of(i * chunk + owner * quarter, quarter), quarter)
+
+    def scatter_copy(i, d):
+        return remote(
+            mine.at[part_rows(i, other(d))], inbox.at[i, d - 1], rs_send.at[i, d - 1], rs_recv.at[i, d - 1], other(d), q
+        )
+
+    def gather_copy(i, d, owner):
+        return remote(
+            total.at[i], top_ref.at[part_rows(i, owner)], ag_send.at[i, d - 1], ag_recv.at[i, d - 1], other(d), q
+        )
+
+    def old_copy(i, d, target):
+        return remote(
+            old.at[part_rows(i, target)], old_ref.at[part_rows(i, target)], old_send.at[i, d - 1], old_recv.at[i], other(d), q
+        )
+
+    def spread_root(i, d):
+        return remote(
+            old.at[part_rows(i, 0)], old_ref.at[part_rows(i, 0)], spread_send.at[i, d - 1], spread_recv.at[i, d - 1], other(d), q
+        )
+
+    def spread_copy(i, d, owner):
+        return remote(
+            old_ref.at[part_rows(i, owner)], old_ref.at[part_rows(i, owner)],
+            spread_send.at[i, d - 1], spread_recv.at[i, d - 1], other(d), q,
+        )
+
+    def panel_copy(d, owner):
+        return remote(panel_ref, slots_ref.at[owner], panel_send.at[d], panel_recv.at[d], p, along(d))
+
+    def sibling_copy():
+        return remote(panel_ref, slots_ref.at[q], panel_send.at[0], panel_recv.at[0], p, sibling)
+
+    def pass_copy(d, owner):
+        return remote(slots_ref.at[owner], slots_ref.at[owner], pass_send.at[d], pass_recv.at[d], p, sibling)
+
+    def corner_down(d):
+        return remote(corner_ref, corner_out_ref, corner_send.at[d - 1], corner_recv.at[0], other(d), q)
+
+    def corner_across(d):
+        return remote(
+            corner_ref, corner_out_ref, corner_send.at[peers + d - 1], corner_recv.at[0], p, lax.rem(q + d, ring)
+        )
+
+    def corner_forward(d):
+        return remote(
+            corner_out_ref, corner_out_ref, corner_send.at[peers + d - 1], corner_recv.at[0], p, lax.rem(q + d, ring)
+        )
+
+    def own_panel():
+        return pltpu.make_async_copy(panel_ref, slots_ref.at[q], local_sem.at[0])
+
+    def own_corner():
+        return pltpu.make_async_copy(corner_ref, corner_out_ref, local_sem.at[1])
+
+    def own_old():
+        return pltpu.make_async_copy(old, old_ref, local_sem.at[2])
+
+    def own_total(i):
+        return pltpu.make_async_copy(total.at[i], top_ref.at[part_rows(i, p)], local_sem.at[3 + i])
+
+    @pl.when(step == 0)
+    def _():
+        barrier = pltpu.get_barrier_semaphore()
+        for d in range(1, peers):
+            pl.semaphore_signal(barrier, inc=1, device_id=(other(d), q), device_id_type=pl.DeviceIdType.MESH)
+        for d in range(1, ring):
+            pl.semaphore_signal(
+                barrier, inc=1, device_id=(p, lax.rem(q + d, ring)), device_id_type=pl.DeviceIdType.MESH
+            )
+        pl.semaphore_wait(barrier, peers + ring - 2)
+        for d in range(1, hops):
+            panel_copy(d, q).start()
+        sibling_copy().start()
+        own_panel().start()
+
+        @pl.when((p == 0) & (q == 0))
+        def _():
+            for d in range(1, peers):
+                corner_down(d).start()
+            for d in range(1, ring):
+                corner_across(d).start()
+            own_corner().start()
+
+        wanted = wanted_rows(pivot_row_ref[...], pivot_col_ref[...])[:1] - p * row_count
+        wanted = jnp.concatenate([wanted[:, :width], wanted[:, :width]], axis=1)
+        row = lax.broadcasted_iota(jnp.int32, choose.shape, 0)
+        choose[...] = (row == wanted).astype(jnp.float32).astype(jnp.bfloat16)
+
+    here = pl.ds(pl.multiple_of(step * chunk, chunk), chunk)
+    found = []
+    for part in range(2):
+        high, low = split(matrix_ref[part])
+        found.append(
+            jnp.dot(high, choose[...], preferred_element_type=jnp.float32)
+            + jnp.dot(low, choose[...], preferred_element_type=jnp.float32)
+        )
+    lane = lax.broadcasted_iota(jnp.int32, (chunk, LANES), 1)
+    mine[here, :] = jnp.where(lane < width, found[0], found[1])
+    for d in range(1, peers):
+        scatter_copy(step, d).start()
+
+    @pl.when(p == 0)
+    def _():
+        old[here, :] = jnp.concatenate([matrix_ref[0, :, :width], matrix_ref[1, :, :width]], axis=1)
+        for d in range(1, peers):
+            old_copy(step, d, d).start()
+        for d in range(1, peers):
+            spread_root(step, d).start()
+
+    def finish(i):
+        for d in range(1, peers):
+            scatter_copy(i, d).wait_recv()
+        summed = mine[part_rows(i, p), :]
+        for d in range(1, peers):
+            summed = summed + inbox[i, d - 1]
+        total[i] = summed
+        for d in range(1, peers):
+            gather_copy(i, d, p).start()
+        own_total(i).start()
+
+        @pl.when(p != 0)
+        def _():
+            old_copy(i, 1, p).wait_recv()
+            for d in range(1, peers):
+                @pl.when(other(d) != 0)
+                def _(d=d):
+                    spread_copy(i, d, p).start()
+
+    @pl.when(step > 0)
+    def _():
+        finish(step - 1)
+
+    @pl.when(step == last)
+    def _():
+        for d in range(1, hops):
+            panel_copy(d, behind(d)).wait_recv()
+            pass_copy(d, behind(d)).start()
+
+        @pl.when((q == 0) & (p != 0))
+        def _():
+            corner_down(1).wait_recv()
+            for d in range(1, ring):
+                corner_forward(d).start()
+
+        finish(last)
+
+        @pl.when(p == 0)
+        def _():
+            own_old().start()
+            own_old().wait()
+
+        @pl.when((p == 0) & (q == 0))
+        def _():
+            own_corner().wait()
+            for d in range(1, peers):
+                corner_down(d).wait_send()
+            for d in range(1, ring):
+                corner_across(d).wait_send()
+
+        @pl.when((p != 0) & (q == 0))
+        def _():
+            for d in range(1, ring):
+                corner_forward(d).wait_send()
+
+        @pl.when(q != 0)
+        def _():
+            corner_across(1).wait_recv()
+
+        own_panel().wait()
+        remote(panel_ref, slots_ref.at[sibling], panel_send.at[0], panel_recv.at[0], p, sibling).wait()
+        for d in range(1, hops):
+            panel_copy(d, q).wait_send()
+            pass_copy(d, behind(d)).wait_send()
+            pass_copy(d, lax.rem(sibling + ring - 2 * d, ring)).wait_recv()
+
+        def drain(i, carry):
+            own_total(i).wait()
+            for d in range(1, peers):
+                scatter_copy(i, d).wait_send()
+                gather_copy(i, d, p).wait_send()
+                gather_copy(i, d, sender(d)).wait_recv()
+
+            @pl.when(p == 0)
+            def _():
+                for d in range(1, peers):
+                    old_copy(i, d, d).wait_send()
+                    spread_root(i, d).wait_send()
+
+            @pl.when(p != 0)
+            def _():
+                for d in range(1, peers):
+                    spread_copy(i, d, sender(d)).wait_recv()
+
+                    @pl.when(other(d) != 0)
+                    def _(d=d):
+                        spread_copy(i, d, p).wait_send()
+
+            return carry
+
+        lax.fori_loop(0, last + 1, drain, 0)
+
+
+def exchange(pivot_row, pivot_col, corner, panel, matrix, chunk):
+    _, columns, rows = matrix.shape
+    peers, ring = lax.axis_size("prow"), lax.axis_size("pcol")
+    steps = columns // chunk
+    quarter = chunk // peers
+    anywhere = pl.BlockSpec(memory_space=pl.ANY)
+    dma = pltpu.SemaphoreType.DMA
+    return pl.pallas_call(
+        lambda *refs: exchange_kernel(peers, ring, *refs),
+        out_shape=(
+            jax.ShapeDtypeStruct((columns, LANES), jnp.float32),
+            jax.ShapeDtypeStruct((columns, LANES), jnp.float32),
+            jax.ShapeDtypeStruct(corner.shape, jnp.float32),
+            jax.ShapeDtypeStruct((ring,) + panel.shape, jnp.float32),
+        ),
+        grid=(steps,),
+        in_specs=[
+            pl.BlockSpec(pivot_row.shape, lambda i: (0, 0)),
+            pl.BlockSpec(pivot_col.shape, lambda i: (0, 0)),
+            anywhere,
+            anywhere,
+            pl.BlockSpec((2, chunk, rows), lambda i: (0, i, 0)),
+        ],
+        out_specs=(anywhere,) * 4,
+        scratch_shapes=[
+            pltpu.VMEM((rows, LANES), jnp.bfloat16),
+            pltpu.VMEM((columns, LANES), jnp.float32),
+            pltpu.VMEM((columns, LANES), jnp.float32),
+            pltpu.VMEM((steps, peers - 1, quarter, LANES), jnp.float32),
+            pltpu.VMEM((steps, quarter, LANES), jnp.float32),
+            dma((steps, peers - 1)), dma((steps, peers - 1)),
+            dma((steps, peers - 1)), dma((steps, peers - 1)),
+            dma((steps, peers - 1)), dma((steps,)),
+            dma((steps, peers - 1)), dma((steps, peers - 1)),
+            dma((ring // 2,)), dma((ring // 2,)),
+            dma((ring // 2,)), dma((ring // 2,)),
+            dma((peers + ring,)), dma((1,)), dma((3 + steps,)),
+        ],
+        compiler_params=pltpu.CompilerParams(
+            vmem_limit_bytes=44 * MIB, collective_id=0, has_side_effects=True
+        ),
+        cost_estimate=pl.CostEstimate(flops=columns * rows * 8 * LANES, bytes_accessed=columns * rows * 8, transcendentals=0),
+    )(pivot_row, pivot_col, corner, panel, matrix)
+
+
+def exchange_plain(pivot_row, pivot_col, corner, panel, matrix):
+    width = panel.shape[1]
+    slots = lax.all_gather(panel, "pcol")
+    mine = (lax.axis_index("prow") == 0) & (lax.axis_index("pcol") == 0)
+    share = panel.shape[2]
+    if share < width:
+        head = jnp.concatenate([slots[k] for k in range(-(-width // share))], axis=2)[:, :, :width]
+        first = jnp.where(lax.axis_index("prow") == 0, head, 0.0)
+        corner = lax.psum(first, "prow")
+    else:
+        corner = lax.psum(jnp.where(mine, panel[:, :, :width], 0.0), ("prow", "pcol"))
+    corner = jnp.concatenate([corner[0], corner[1]], axis=1)
+    slab = lax.psum(pick(pivot_row, pivot_col, matrix), "prow")
+    top = jnp.concatenate([slab[0, :, :width], slab[1, :, :width]], axis=1)
+    old = jnp.concatenate([slab[0, :, width:], slab[1, :, width:]], axis=1)
+    slots = jnp.moveaxis(slots, 0, 2).reshape(1, 2, width, -1)
+    return top, old, corner, slots
+
+
 def on_device(matrix, panel_lower, pivot_rows):
     width = pivot_rows.shape[0]
+    share = panel_lower.shape[2]
+    columns = matrix.shape[1]
+    peers, ring = lax.axis_size("prow"), lax.axis_size("pcol")
     pivot_row = jnp.pad(pivot_rows, (0, LANES - width), constant_values=-1).reshape(1, LANES)
     pivot_col = pivot_rows.reshape(width, 1)
-    gathered = lax.all_gather(panel_lower, "pcol", axis=2, tiled=True)
-    corner = lax.psum(jnp.where(lax.axis_index("prow") == 0, gathered[:, :, :width], 0.0), "prow")
-    picked = pick(pivot_row, pivot_col, matrix)
-    slab = lax.psum(picked, "prow")
-    left, right, keep = prepare(pivot_col, slab, corner, gathered)
+    chunk = largest_divisor(columns, 256, 16)
+    if share % width == 0 and ring <= 8 and chunk % (8 * peers) == 0:
+        corner = jnp.concatenate([panel_lower[0, :, :width], panel_lower[1, :, :width]], axis=1)
+        moved = exchange(pivot_row, pivot_col, corner, panel_lower, matrix, chunk)
+    else:
+        moved = exchange_plain(pivot_row, pivot_col, None, panel_lower, matrix)
+    left, right, keep = prepare(pivot_col, *moved)
     return update(left, right, keep, matrix)
 
 

time: 173 us -> 103 us (0.60)
  waiting for transfers between devices: 47 us -> 0 us
  blocking collectives: 16.9 us -> 0 us
  Pallas kernels: 84.1 us -> 99.3 us
  between operations: 14.9 us -> 0.02 us
  local copies, waits for them, and re-layouts: 9.22 us -> 3.13 us
    psum x1 -> x0, waiting for transfers between devices: 34.6 us -> none  [on_device(): slab = lax.psum(picked, 'prow')]
    pallas_call x2, Pallas kernels: 38.9 us -> 58.1 us  [the longest x1 53.2 us: exchange(): pl.pallas_call(lambda *refs: exchange_kernel(peers, ring, *refs), out_sha...]
    psum x1 -> x0, blocking collectives: 16.9 us -> none  [on_device(): lax.psum(jnp.where(lax.axis_index('prow') == 0, gathered[:, :, :width], 0...]
    all_gather x1 -> x0, waiting for transfers between devices: 12.3 us -> none  [on_device(): gathered = lax.all_gather(panel_lower, 'pcol', axis=2, tiled=True)]
    all_gather x1 -> x0, local copies, waits for them, and re-layouts: 4.37 us -> none  [on_device(): gathered = lax.all_gather(panel_lower, 'pcol', axis=2, tiled=True)]
    pallas_call x1, Pallas kernels: 45.2 us -> 41.2 us  [update(): pl.pallas_call(update_kernel, out_shape=jax.ShapeDtypeStruct(matrix.shape...]
    unnamed x3 -> x2, local copies, waits for them, and re-layouts: 3.45 us -> 0.95 us
  transfers between devices with their start and end apart: 2 -> 0, of which waited for: 2 -> 0; matrix products, arithmetic and copies ran while one was open for 3% -> 0% of each run, Pallas kernels for 19% -> 0%
where the time goes in v2:
time: 103 us
  Pallas kernels  99.3 us (96%)
  local copies, waits for them, and re-layouts  3.13 us (3%)
    pallas_call x1, Pallas kernels, exchange(): pl.pallas_call(lambda *refs: exchange_kernel(peers, ring, *refs), out_sha...  53.2 us
    pallas_call x1, Pallas kernels, update(): pl.pallas_call(update_kernel, out_shape=jax.ShapeDtypeStruct(matrix.shape...  41.2 us
    pallas_call x1, Pallas kernels, prepare(): pl.pallas_call(prepare_kernel, out_shape=(jax.ShapeDtypeStruct((2, column...  4.94 us

profile of v2, /device:TPU:0, one launch (start us, length us, event | category | flops | bytes accessed | tf_op | source)
XLA Modules:
  0.0 102.6 jit_solution(4895491143176529988)
XLA Ops:
  0.0 0.7 pad_bitcast_fusion.refs_0_
  0.7 0.7 copy.5.refs_1_.pivot_col_ref
  1.4 0.8 slice_bitcast_fusion.1
  2.2 0.1 pad_maximum_fusion.refs_2_
  2.3 0.0 copy-start
  2.3 1.0 copy-done
  3.2 53.2 %shard_map.37 = (f32[1792,128]{1,0:T(8,128)S(1)}, f32[1792,128]{1,0:T(8,128)S(1)}, f32[64,128]{1,0:T(8,128)S(1)}, f32[8,2,64,448]{3,2,1,0:T(8,128)S(1)}) custom-call(s32[1,128]{1,0:T(1,128)S(1)} %pad_bitcast_fusion.refs_0_, s32[64,1]{1,0:T(8,128)S(1)} %copy.5.refs_1_.pivot_col_ref, f32[64,128]{1,0:T(8,128)S(1)} %pad_maximum_fusion.refs_2_, ...), custom_call_target="tpu_custom_call" | custom-call | flops 6576668672 | bytes 51380224 | tf_op jit(solution)/shard_map/pallas_call | solution.py:469
  56.4 4.9 %shard_map.38 = (bf16[2,1792,512]{2,1,0:T(8,128)(2,1)S(1)}, bf16[2,512,3584]{2,1,0:T(8,128)(2,1)S(1)}, f32[8,3584]{1,0:T(8,128)S(1)}) custom-call(s32[64,1]{1,0:T(8,128)S(1)} %copy.5.refs_1_.pivot_col_ref, f32[1792,128]{1,0:T(8,128)S(1)} %get-tuple-element.12.top_ref, f32[1792,128]{1,0:T(8,128)S(1)} %get-tuple-element.13.old_ref, ...), custom_call_target="tpu_custom_call" | custom-call | tf_op jit(solution)/shard_map/pallas_call | solution.py:180
  61.4 41.2 %shard_map.39 = f32[2,1792,3584]{2,1,0:T(8,128)} custom-call(bf16[2,1792,512]{2,1,0:T(8,128)(2,1)S(1)} %get-tuple-element.16.left_ref, bf16[2,512,3584]{2,1,0:T(8,128)(2,1)S(1)} %get-tuple-element.17.right_ref, f32[8,3584]{1,0:T(8,128)S(1)} %get-tuple-element.18.keep_ref, f32[2,1792,3584]{2,1,0:T(8,128)} %matrix_ref.1), custom_call_target="tpu_custom_call" | custom-call | tf_op jit(solution)/shard_map/pallas_call | solution.py:207
Async XLA Ops:
  2.3 1.0 copy-start

commit v3 on v2

--- a/solution.py
+++ b/solution.py
@@ -186,42 +186,75 @@
         ),
         in_specs=[whole] * 5,
         out_specs=(whole,) * 3,
-        compiler_params=pltpu.CompilerParams(vmem_limit_bytes=32 * MIB),
+        compiler_params=pltpu.CompilerParams(vmem_limit_bytes=12 * MIB),
     )(pivot_col, top, old, corner, panel)
 
 
-def update_kernel(left_ref, right_ref, keep_ref, matrix_ref, out_ref):
-    columns = matrix_ref.shape[1]
-    chunk = largest_divisor(columns, 896, 16)
+def columns_held(matrix):
+    rows = matrix.shape[2]
+    span = largest_divisor(rows, 2 * LANES, LANES)
+    return span * (rows // span * 5 // 14)
+
+
+def update_kernel(held_steps, left_ref, right_ref, keep_ref, *refs):
+    *sources, out_ref = refs
+    columns = out_ref.shape[1]
+    rows = pl.ds(pl.multiple_of(pl.program_id(1) * columns, 16), columns)
     keep = keep_ref[:1, :] > 0.5
-    for part in range(2):
-        for start in range(0, columns, chunk):
-            rows = slice(start, start + chunk)
+
+    def apply(source):
+        for part in range(2):
             product = jnp.dot(left_ref[part, rows, :], right_ref[part], preferred_element_type=jnp.float32)
-            out_ref[part, rows, :] = jnp.where(keep, matrix_ref[part, rows, :], 0.0) + product
-
-
-def update(left, right, keep, matrix):
+            out_ref[part] = jnp.where(keep, source[part], 0.0) + product
+
+    if held_steps == 0:
+        apply(sources[0])
+        return
+
+    @pl.when(pl.program_id(0) < held_steps)
+    def _():
+        apply(sources[1])
+
+    @pl.when(pl.program_id(0) >= held_steps)
+    def _():
+        apply(sources[0])
+
+
+def update(left, right, keep, matrix, kept):
     _, columns, rows = matrix.shape
     span = largest_divisor(rows, 2 * LANES, LANES)
+    held_steps = 0 if kept is None else kept.shape[2] // span
+    chunk = largest_divisor(columns, 896, 16)
+    parts = columns // chunk
+    sources = [matrix]
+    if kept is not None:
+        sources.append(pltpu.with_memory_space_constraint(kept, pltpu.VMEM))
+    source_specs = [
+        pl.BlockSpec(
+            (2, chunk, span), lambda j, i: (0, jnp.where(j < held_steps, 0, i), jnp.maximum(j, held_steps))
+        ),
+        pl.BlockSpec(
+            (2, chunk, span),
+            lambda j, i: (0, jnp.where(j < held_steps, i, parts - 1), jnp.minimum(j, held_steps - 1)),
+        ),
+    ]
     return pl.pallas_call(
-        update_kernel,
+        lambda *refs: update_kernel(held_steps, *refs),
         out_shape=jax.ShapeDtypeStruct(matrix.shape, jnp.float32),
-        grid=(rows // span,),
+        grid=(rows // span, parts),
         in_specs=[
-            pl.BlockSpec(left.shape, lambda j: (0, 0, 0), pipeline_mode=pl.Buffered(1)),
-            pl.BlockSpec((2, right.shape[1], span), lambda j: (0, 0, j)),
-            pl.BlockSpec((8, span), lambda j: (0, j)),
-            pl.BlockSpec((2, columns, span), lambda j: (0, 0, j)),
-        ],
-        out_specs=pl.BlockSpec((2, columns, span), lambda j: (0, 0, j)),
-        compiler_params=pltpu.CompilerParams(vmem_limit_bytes=40 * MIB),
-    )(left, right, keep, matrix)
+            pl.BlockSpec(left.shape, lambda j, i: (0, 0, 0), pipeline_mode=pl.Buffered(1)),
+            pl.BlockSpec((2, right.shape[1], span), lambda j, i: (0, 0, j)),
+            pl.BlockSpec((8, span), lambda j, i: (0, j)),
+        ] + source_specs[: len(sources)],
+        out_specs=pl.BlockSpec((2, chunk, span), lambda j, i: (0, i, j)),
+        compiler_params=pltpu.CompilerParams(vmem_limit_bytes=22 * MIB),
+    )(left, right, keep, *sources)
 
 
 def exchange_kernel(
     peers, ring, pivot_row_ref, pivot_col_ref, corner_ref, panel_ref, matrix_ref,
-    top_ref, old_ref, corner_out_ref, slots_ref,
+    top_ref, old_ref, corner_out_ref, slots_ref, kept_ref,
     choose, mine, old, inbox, total,
     rs_send, rs_recv, ag_send, ag_recv, old_send, old_recv, spread_send, spread_recv,
     panel_send, panel_recv, pass_send, pass_recv, corner_send, corner_recv, local_sem,
@@ -346,6 +379,11 @@
         choose[...] = (row == wanted).astype(jnp.float32).astype(jnp.bfloat16)
 
     here = pl.ds(pl.multiple_of(step * chunk, chunk), chunk)
+    held = kept_ref.shape[2]
+    keep_copy = pltpu.make_async_copy(
+        matrix_ref.at[:, :, pl.ds(0, held)], kept_ref.at[:, here, :], local_sem.at[3 + last + 1]
+    )
+    keep_copy.start()
     found = []
     for part in range(2):
         high, low = split(matrix_ref[part])
@@ -389,6 +427,8 @@
     def _():
         finish(step - 1)
 
+    keep_copy.wait()
+
     @pl.when(step == last)
     def _():
         for d in range(1, hops):
@@ -459,7 +499,7 @@
         lax.fori_loop(0, last + 1, drain, 0)
 
 
-def exchange(pivot_row, pivot_col, corner, panel, matrix, chunk):
+def exchange(pivot_row, pivot_col, corner, panel, matrix, chunk, held):
     _, columns, rows = matrix.shape
     peers, ring = lax.axis_size("prow"), lax.axis_size("pcol")
     steps = columns // chunk
@@ -473,6 +513,7 @@
             jax.ShapeDtypeStruct((columns, LANES), jnp.float32),
             jax.ShapeDtypeStruct(corner.shape, jnp.float32),
             jax.ShapeDtypeStruct((ring,) + panel.shape, jnp.float32),
+            pltpu.VMEM((2, columns, held), jnp.float32),
         ),
         grid=(steps,),
         in_specs=[
@@ -482,7 +523,7 @@
             anywhere,
             pl.BlockSpec((2, chunk, rows), lambda i: (0, i, 0)),
         ],
-        out_specs=(anywhere,) * 4,
+        out_specs=(anywhere,) * 5,
         scratch_shapes=[
             pltpu.VMEM((rows, LANES), jnp.bfloat16),
             pltpu.VMEM((columns, LANES), jnp.float32),
@@ -495,10 +536,10 @@
             dma((steps, peers - 1)), dma((steps, peers - 1)),
             dma((ring // 2,)), dma((ring // 2,)),
             dma((ring // 2,)), dma((ring // 2,)),
-            dma((peers + ring,)), dma((1,)), dma((3 + steps,)),
+            dma((peers + ring,)), dma((1,)), dma((4 + steps,)),
         ],
         compiler_params=pltpu.CompilerParams(
-            vmem_limit_bytes=44 * MIB, collective_id=0, has_side_effects=True
+            vmem_limit_bytes=34 * MIB, collective_id=0, has_side_effects=True
         ),
         cost_estimate=pl.CostEstimate(flops=columns * rows * 8 * LANES, bytes_accessed=columns * rows * 8, transcendentals=0),
     )(pivot_row, pivot_col, corner, panel, matrix)
@@ -533,11 +574,11 @@
     chunk = largest_divisor(columns, 256, 16)
     if share % width == 0 and ring <= 8 and chunk % (8 * peers) == 0:
         corner = jnp.concatenate([panel_lower[0, :, :width], panel_lower[1, :, :width]], axis=1)
-        moved = exchange(pivot_row, pivot_col, corner, panel_lower, matrix, chunk)
+        *moved, kept = exchange(pivot_row, pivot_col, corner, panel_lower, matrix, chunk, columns_held(matrix))
     else:
-        moved = exchange_plain(pivot_row, pivot_col, None, panel_lower, matrix)
+        moved, kept = exchange_plain(pivot_row, pivot_col, None, panel_lower, matrix), None
     left, right, keep = prepare(pivot_col, *moved)
-    return update(left, right, keep, matrix)
+    return update(left, right, keep, matrix, kept)
 
 
 def solution(mesh):

time: 103 us -> 121 us (1.17)
  local copies, waits for them, and re-layouts: 3.13 us -> 17.6 us
  Pallas kernels: 99.3 us -> 102 us
    unnamed x2 -> x8, local copies, waits for them, and re-layouts: 0.95 us -> 15.4 us
    pallas_call x1, Pallas kernels: 41.2 us -> 43.8 us  [update(): pl.pallas_call(lambda *refs: update_kernel(held_steps, *refs), out_shape=...]
where the time goes in v3:
time: 121 us; the launch traced here: 120 us
  Pallas kernels  102 us (84%)
  local copies, waits for them, and re-layouts  17.6 us (15%)
    pallas_call x1, Pallas kernels, exchange(): pl.pallas_call(lambda *refs: exchange_kernel(peers, ring, *refs), out_sha...  53.4 us
    pallas_call x1, Pallas kernels, update(): pl.pallas_call(lambda *refs: update_kernel(held_steps, *refs), out_shape=...  43.8 us
    unnamed x8, local copies, waits for them, and re-layouts  15.4 us
    pallas_call x1, Pallas kernels, prepare(): pl.pallas_call(prepare_kernel, out_shape=(jax.ShapeDtypeStruct((2, column...  4.94 us

profile of v3, /device:TPU:0, one launch (start us, length us, event | category | flops | bytes accessed | tf_op | source)
XLA Modules:
  0.0 119.9 jit_solution(15910586299901214619)
XLA Ops:
  0.0 0.7 pad_bitcast_fusion.refs_0_
  0.7 0.7 copy.5.refs_1_.pivot_col_ref
  1.4 0.8 slice_bitcast_fusion.1
  2.2 0.1 pad_maximum_fusion.refs_2_
  2.3 0.0 copy-start.3
  2.3 1.0 copy-done.3
  3.2 53.4 %shard_map.37 = (f32[1792,128]{1,0:T(8,128)S(1)}, f32[1792,128]{1,0:T(8,128)S(1)}, f32[64,128]{1,0:T(8,128)S(1)}, f32[8,2,64,448]{3,2,1,0:T(8,128)}, f32[2,1792,1280]{2,1,0:T(8,128)S(1)}) custom-call(s32[1,128]{1,0:T(1,128)S(1)} %pad_bitcast_fusion.refs_0_, s32[64,1]{1,0:T(8,128)S(1)} %copy.5.refs_1_.pivot_col_ref, f32[64,128]{1,0:T(8,128)S(1)} %pad_maximum_fusion.refs_2_, ...), custom_call_target="tpu_custom_call" | custom-call | flops 6576668672 | bytes 51380224 | tf_op jit(solution)/shard_map/pallas_call | solution.py:509
  56.7 0.0 copy-start
  56.7 6.7 %copy-done = f32[2,1792,1280]{2,1,0:T(8,128)} copy-done((f32[2,1792,1280]{2,1,0:T(8,128)}, f32[2,1792,1280]{2,1,0:T(8,128)S(1)}, u32[]{:S(2)}) %copy-start) | copy-done | bytes 18350104
  63.3 0.0 copy-start.2
  63.3 1.6 %copy-done.2 = f32[8,2,64,448]{3,2,1,0:T(8,128)S(1)} copy-done((f32[8,2,64,448]{3,2,1,0:T(8,128)S(1)}, f32[8,2,64,448]{3,2,1,0:T(8,128)}, u32[]{:S(2)}) %copy-start.2) | copy-done | bytes 1835032
  64.9 4.9 %shard_map.38 = (bf16[2,1792,512]{2,1,0:T(8,128)(2,1)S(1)}, bf16[2,512,3584]{2,1,0:T(8,128)(2,1)S(1)}, f32[8,3584]{1,0:T(8,128)S(1)}) custom-call(s32[64,1]{1,0:T(8,128)S(1)} %copy.5.refs_1_.pivot_col_ref, f32[1792,128]{1,0:T(8,128)S(1)} %get-tuple-element.13.top_ref, f32[1792,128]{1,0:T(8,128)S(1)} %get-tuple-element.14.old_ref, ...), custom_call_target="tpu_custom_call" | custom-call | tf_op jit(solution)/shard_map/pallas_call | solution.py:180
  69.9 0.0 copy-start.1
  69.9 6.2 %copy-done.1 = f32[2,1792,1280]{2,1,0:T(8,128)S(1)} copy-done((f32[2,1792,1280]{2,1,0:T(8,128)S(1)}, f32[2,1792,1280]{2,1,0:T(8,128)}, u32[]{:S(2)}) %copy-start.1) | copy-done | bytes 18350104
  76.1 43.8 %shard_map.39 = f32[2,1792,3584]{2,1,0:T(8,128)} custom-call(bf16[2,1792,512]{2,1,0:T(8,128)(2,1)S(1)} %get-tuple-element.17.refs_0_, bf16[2,512,3584]{2,1,0:T(8,128)(2,1)S(1)} %get-tuple-element.18.refs_1_, f32[8,3584]{1,0:T(8,128)S(1)} %get-tuple-element.19.refs_2_, f32[2,1792,3584]{2,1,0:T(8,128)} %refs_3_.3, f32[2,1792,1280]{2,1,0:T(8,128)S(1)} %copy-done.1), custom_call_target="tpu_custom_call" | custom-call | tf_op jit(solution)/shard_map/pallas_call | solution.py:241
Async XLA Ops:
  2.3 1.0 copy-start.3
  56.7 6.7 %copy-start = (f32[2,1792,1280]{2,1,0:T(8,128)}, f32[2,1792,1280]{2,1,0:T(8,128)S(1)}, u32[]{:S(2)}) copy-start(f32[2,1792,1280]{2,1,0:T(8,128)S(1)} %get-tuple-element.20.refs_4_) | copy-start | bytes 55050244
  63.3 1.6 %copy-start.2 = (f32[8,2,64,448]{3,2,1,0:T(8,128)S(1)}, f32[8,2,64,448]{3,2,1,0:T(8,128)}, u32[]{:S(2)}) copy-start(f32[8,2,64,448]{3,2,1,0:T(8,128)} %get-tuple-element.16.panel_ref) | copy-start | bytes 5505028
  69.9 6.2 %copy-start.1 = (f32[2,1792,1280]{2,1,0:T(8,128)S(1)}, f32[2,1792,1280]{2,1,0:T(8,128)}, u32[]{:S(2)}) copy-start(f32[2,1792,1280]{2,1,0:T(8,128)} %copy-done) | copy-start | bytes 55050244
